TPU v7x, 32 devices: a whole 2x2x4 slice. The times are simulated.
32 devices in a mesh: groups: 2 (over y), expert: 4 (over z), parent: 2 (over x), dp: 2 (over core).
Axes of the slice: x: 2, y: 2, z: 4, core: 2. Of those that a mesh axis runs over, the one named last changes fastest.
Arguments:
- activations: bfloat16 [512, 5120], P(('groups', 'dp'), 'expert'), parts along dimension 0, may hold values from -6 to 6
- parent_encoder: bfloat16 [5120, 8192], P('expert', 'parent'), may hold values from -0.078125 to 0.078125
- parent_bias: float32 [8192], P('parent'), may hold values from -0.5 to 0.5
- parent_decoder: bfloat16 [8192, 5120], P('parent', 'expert'), may hold values from -0.0625 to 0.0625
- child_encoder: bfloat16 [8, 5120, 128], P(('expert', 'parent')), may hold values from -0.078125 to 0.078125
- child_bias: float32 [8, 128], P(('expert', 'parent')), may hold values from -0.5 to 0.5
- child_decoder: bfloat16 [8, 128, 5120], P(('expert', 'parent')), may hold values from -0.5 to 0.5
- child_blocks: int32 [512, 1], P(('groups', 'dp')), parts along dimension 0, may hold values from 0 to 7; in each aligned block of 32 rows (0 to 31, 32 to 63, ...) at most 10 rows name the same one
- block_owner: int32 [8], replicated, may hold values from 0 to 3, as said below
Outputs:
- reconstruction: bfloat16 [512, 5120], P(('groups', 'dp'), 'expert'), parts along dimension 0
- child_encoder_grad: bfloat16 [16, 5120, 128], P(('groups', 'expert', 'parent'), 'dp'), parts along dimension 0
- child_decoder_grad: bfloat16 [16, 128, 5120], P(('groups', 'expert', 'parent'), None, 'dp'), parts along dimension 0
There are 2 independent parts, one for each index of `groups`. A program takes and returns all parts, laid end to end along the dimension named above; an argument that names none is the same for every part. Nothing has to cross between parts.
Inputs may be any that keep to these rules, and one draw needn't show every extreme that they name: `child_blocks`: each row names 1 different child blocks; in each aligned block of 32 rows no child block is named by more than 10 rows, and some child block is named by exactly 10. `block_owner`: for each parent index q, the entries q * 4 to (q + 1) * 4 - 1 name every owner once.
All inputs are finite; a program needn't handle non-finite values.
Results may differ from a plain program's by a relative error of at most 0.011.
Values may be sent and summed in bfloat16 or wider, within the bound.
A program may use at most 128 MiB of HBM per device.

v0:
```python
import jax
import jax.numpy as jnp
from jax import lax
from jax.sharding import PartitionSpec as P

CAP = 10


ERROR_SCALE = 0.03125


def body(
    activations,
    parent_encoder,
    parent_bias,
    parent_decoder,
    child_encoder,
    child_bias,
    child_decoder,
    child_blocks,
    block_owner,
):
    owners = lax.axis_size("expert")
    my_owner = lax.axis_index("expert")
    my_shard = lax.axis_index("parent")
    local_rows, columns = activations.shape
    source_rows = local_rows // owners
    per_shard = parent_encoder.shape[1]
    stride = per_shard // owners
    highest = lax.Precision.HIGHEST
    partial_value = jnp.dot(activations, parent_encoder, preferred_element_type=jnp.float32)
    parent_linear = lax.psum(partial_value, "expert") + parent_bias
    parent_active = jnp.maximum(parent_linear, 0.0).astype(jnp.bfloat16)
    parent_gates = (
        parent_active[:, ::stride].astype(jnp.float32).reshape(owners, source_rows, owners)
    )
    local_blocks = my_shard * owners + jnp.arange(owners, dtype=jnp.int32)
    owners_here = lax.dynamic_slice_in_dim(block_owner, my_shard * owners, owners)
    owner_onehot = (owners_here[:, None] == jnp.arange(owners, dtype=jnp.int32)[None, :]).astype(
        jnp.float32
    )
    owner_column = (owners_here == my_owner).astype(jnp.float32)
    named_blocks = child_blocks.reshape(owners, source_rows, -1)
    block_hits = jnp.sum((named_blocks[..., None] == local_blocks).astype(jnp.int32), axis=2)
    slot_ranks = jnp.cumsum(block_hits, axis=1) - block_hits
    slot_hits = (
        block_hits[..., None]
        * (slot_ranks[..., None] == jnp.arange(CAP, dtype=jnp.int32)).astype(jnp.int32)
    ).astype(jnp.float32)
    selection = jnp.einsum("sijc,jo->soci", slot_hits, owner_onehot, precision=highest).astype(
        jnp.bfloat16
    )
    own_selection = jnp.einsum("sijc,j->sci", slot_hits, owner_column, precision=highest)
    gate_rows = jnp.einsum("sij,j->si", parent_gates, owner_column, precision=highest)
    slot_gate = jnp.einsum("sci,si->sc", own_selection, gate_rows, precision=highest)
    own_table = lax.dynamic_index_in_dim(selection, my_owner, 0, keepdims=False)

    def send_slots(values):
        whole_rows = lax.all_to_all(values, "expert", split_axis=0, concat_axis=1, tiled=True)
        packed = jnp.einsum(
            "oci,id->ocd", own_table, whole_rows, preferred_element_type=jnp.float32
        ).astype(jnp.bfloat16)
        return lax.all_to_all(packed, "expert", split_axis=0, concat_axis=0, tiled=True)

    input_slots = send_slots(activations)
    encoder_block = child_encoder[0]
    decoder_block = child_decoder[0]
    child_linear = (
        jnp.einsum("scd,dh->sch", input_slots, encoder_block, preferred_element_type=jnp.float32)
        + child_bias[0]
    )
    positive = jnp.maximum(child_linear, 0.0)
    child_active = (positive * positive * slot_gate[..., None]).astype(jnp.bfloat16)
    child_output = jnp.einsum(
        "sch,hd->scd", child_active, decoder_block, preferred_element_type=jnp.float32
    ).astype(jnp.bfloat16)
    returned = lax.all_to_all(child_output, "expert", split_axis=0, concat_axis=0, tiled=True)
    summed = jnp.einsum("oci,ocd->id", own_table, returned, preferred_element_type=jnp.float32)
    child_part = lax.all_to_all(
        summed.astype(jnp.bfloat16), "expert", split_axis=1, concat_axis=0, tiled=True
    ).astype(summed.dtype)
    total_part = (
        jnp.dot(parent_active, parent_decoder, preferred_element_type=jnp.float32) + child_part
    )
    total_sum = lax.psum(total_part, "parent")
    reconstruction = total_sum.astype(jnp.bfloat16)
    scaled_error = ((total_sum - activations.astype(jnp.float32)) * ERROR_SCALE).astype(
        jnp.bfloat16
    )
    error_slots = send_slots(scaled_error)
    decoder_grad = jnp.einsum(
        "sch,scd->hd", child_active, error_slots, preferred_element_type=jnp.float32
    )
    active_grad = jnp.einsum(
        "scd,hd->sch", error_slots, decoder_block, preferred_element_type=jnp.float32
    )
    linear_grad = (active_grad * slot_gate[..., None] * 2.0 * positive).astype(jnp.bfloat16)
    encoder_grad = jnp.einsum(
        "scd,sch->dh", input_slots, linear_grad, preferred_element_type=jnp.float32
    )
    encoder_sum, decoder_sum = (
        lax.psum_scatter(
            encoder_grad[None].astype(jnp.bfloat16), "dp", scatter_dimension=1, tiled=True
        ).astype(jnp.float32),
        lax.psum_scatter(
            decoder_grad[None].astype(jnp.bfloat16), "dp", scatter_dimension=2, tiled=True
        ).astype(jnp.float32),
    )
    return (reconstruction, encoder_sum.astype(jnp.bfloat16), decoder_sum.astype(jnp.bfloat16))


def solution(mesh):
    in_specs = (
        P(("groups", "dp"), "expert"),
        P("expert", "parent"),
        P("parent"),
        P("parent", "expert"),
        P(("expert", "parent"), None, None),
        P(("expert", "parent"), None),
        P(("expert", "parent"), None, None),
        P(("groups", "dp"), None),
        P(),
    )
    out_specs = (
        P(("groups", "dp"), "expert"),
        P(("groups", "expert", "parent"), "dp", None),
        P(("groups", "expert", "parent"), None, "dp"),
    )
    return jax.shard_map(body, mesh=mesh, in_specs=in_specs, out_specs=out_specs, check_vma=False)
```

profile of v0, /device:TPU:0, one launch (start us, length us, event | category | flops | bytes accessed | tf_op | source)
XLA Modules:
  0.0 260.3 jit_solution(4814087544873757390)
XLA Ops:
  7.2 0.0 all-reduce.3.cloned.1.call-start
  7.2 7.0 %fusion.63 = f32[128,4096]{1,0:T(8,128)} fusion(bf16[128,1280]{1,0:T(8,128)(2,1)} %param.9, bf16[1280,4096]{1,0:T(8,128)(2,1)} %param.10), kind=kOutput, calls=%fused_computation.65 | convolution fusion | flops 1342177280 | bytes 12910592 | tf_op jit(solution)/shard_map/dot_general | solution.py:31
  14.3 6.3 %all-to-all-start = ((bf16[4,32,1280]{2,1,0:T(8,128)(2,1)}), bf16[4,32,1280]{2,1,0:T(8,128)(2,1)S(1)}, u32[]{:S(2)}, u32[]{:S(2)}) async-start(bf16[4,32,1280]{2,1,0:T(8,128)(2,1)} %bitcast.5), calls=%async_computation | async-start | bytes 655360 | tf_op jit(solution)/shard_map/all_to_all | solution.py:59
  20.6 0.5 broadcast.52
  21.1 0.7 reduce.3
  21.8 0.1 eq.64
  21.9 0.1 compare_convert_fusion
  22.0 0.1 reduce_window_sum.11
  22.0 0.1 copy.21
  22.1 0.1 fusion.44
  22.2 0.1 copy.20
  22.3 0.1 dynamic_slice.7
  22.4 0.2 fusion.32
  22.6 17.5 %all-to-all-done = bf16[4,32,1280]{2,1,0:T(8,128)(2,1)S(1)} async-done(((bf16[4,32,1280]{2,1,0:T(8,128)(2,1)}), bf16[4,32,1280]{2,1,0:T(8,128)(2,1)S(1)}, u32[]{:S(2)}, u32[]{:S(2)}) %all-to-all-start) | async-done | bytes 327712 | tf_op jit(solution)/shard_map/all_to_all | solution.py:59
  40.2 0.3 copy.22
  40.4 0.2 reshape.52
  40.7 1.2 convolution_convert_fusion.2
  41.9 3.5 %all-to-all-start.1 = ((bf16[4,10,5120]{2,1,0:T(8,128)(2,1)}), bf16[4,10,5120]{2,1,0:T(8,128)(2,1)S(1)}, u32[]{:S(2)}, u32[]{:S(2)}) async-start(bf16[4,10,5120]{2,1,0:T(8,128)(2,1)} %convolution_convert_fusion.2), calls=%async_computation.1 | async-start | bytes 1310720 | tf_op jit(solution)/shard_map/all_to_all | solution.py:63
  45.4 0.0 all-reduce.5.cloned.1.call-start
  45.4 0.2 fusion.30
  45.6 0.1 copy.30
  45.7 30.3 %all-to-all-done.1 = bf16[4,10,5120]{2,1,0:T(8,128)(2,1)S(1)} async-done(((bf16[4,10,5120]{2,1,0:T(8,128)(2,1)}), bf16[4,10,5120]{2,1,0:T(8,128)(2,1)S(1)}, u32[]{:S(2)}, u32[]{:S(2)}) %all-to-all-start.1) | async-done | bytes 409632 | tf_op jit(solution)/shard_map/all_to_all | solution.py:63
  76.0 0.4 fusion.13
  76.4 46.8 %all-reduce.3.cloned.1.call-done = f32[128,4096]{1,0:T(8,128)} async-done(((f32[128,4096]{1,0:T(8,128)}), f32[128,4096]{1,0:T(8,128)}) %all-reduce.3.cloned.1.call-update) | async-done | bytes 2097168 | tf_op jit(solution)/shard_map/psum | solution.py:32
  123.1 1.8 maximum_convert_fusion
  124.9 0.1 slice.3
  125.1 0.1 convolution_bitcast_fusion.3
  125.2 0.2 fusion.36
  125.4 0.4 convolution_convert_fusion.1
  125.8 20.0 %all_to_all.66 = bf16[4,10,5120]{2,1,0:T(8,128)(2,1)S(1)} all-to-all(bf16[4,10,5120]{2,1,0:T(8,128)(2,1)S(1)} %convolution_convert_fusion.1), channel_id=1, replica_groups=mesh['groups'=2,'expert'=4,'parent'=2,'dp'=2] {'expert'}, dimensions={0} | all-to-all | bytes 819200 | tf_op jit(solution)/shard_map/all_to_all | solution.py:77
  145.8 0.3 fusion.4
  146.1 12.3 %all_to_all.67 = bf16[32,4,1280]{2,0,1:T(8,128)(2,1)S(1)} all-to-all(bf16[32,4,1280]{2,0,1:T(8,128)(2,1)S(1)} %bitcast.102), channel_id=1, replica_groups=mesh['groups'=2,'expert'=4,'parent'=2,'dp'=2] {'expert'}, dimensions={1} | all-to-all | bytes 655360 | tf_op jit(solution)/shard_map/all_to_all | solution.py:79
  158.5 6.4 %convolution_add_fusion = f32[128,1280]{1,0:T(8,128)} fusion(f32[128,1280]{1,0:T(8,128)S(1)} %bitcast.99, bf16[128,4096]{1,0:T(8,128)(2,1)S(1)} %maximum_convert_fusion, bf16[4096,1280]{1,0:T(8,128)(2,1)} %param.12), kind=kOutput, calls=%fused_computation.11 | convolution fusion | flops 1342341120 | bytes 12845056 | tf_op jit(solution)/shard_map/dot_general | solution.py:83
  164.8 0.0 all-reduce.5.cloned.1.call-update
  164.9 0.0 reduce-scatter.5.cloned.1.call-start
  164.9 30.6 %all-reduce.5.cloned.1.call-done = f32[128,1280]{1,0:T(8,128)} async-done(((f32[128,1280]{1,0:T(8,128)}), f32[128,1280]{1,0:T(8,128)}) %all-reduce.5.cloned.1.call-update) | async-done | bytes 655376 | tf_op jit(solution)/shard_map/psum | solution.py:85
  195.5 2.2 multiply_convert_fusion
  197.7 14.7 %all_to_all.68 = bf16[4,32,1280]{2,1,0:T(8,128)(2,1)S(1)} all-to-all(bf16[4,32,1280]{2,1,0:T(8,128)(2,1)S(1)} %bitcast.104), channel_id=1, replica_groups=mesh['groups'=2,'expert'=4,'parent'=2,'dp'=2] {'expert'}, dimensions={0} | all-to-all | bytes 655360 | tf_op jit(solution)/shard_map/all_to_all | solution.py:59
  212.4 0.3 copy.26
  212.6 0.2 reshape.62
  212.9 0.3 convolution_convert_fusion
  213.2 19.1 %all_to_all.69 = bf16[4,10,5120]{2,1,0:T(8,128)(2,1)S(1)} all-to-all(bf16[4,10,5120]{2,1,0:T(8,128)(2,1)S(1)} %convolution_convert_fusion), channel_id=1, replica_groups=mesh['groups'=2,'expert'=4,'parent'=2,'dp'=2] {'expert'}, dimensions={0} | all-to-all | bytes 819200 | tf_op jit(solution)/shard_map/all_to_all | solution.py:63
  232.2 1.7 fusion.2
  233.9 0.0 reduce-scatter.5.cloned.1.call-update
  233.9 0.0 reduce-scatter.3.cloned.1.call-start
  234.0 2.7 %fusion.3 = bf16[1,5120,128]{2,1,0:T(8,128)(2,1)} fusion(bf16[4,10,5120]{2,1,0:T(8,128)(2,1)S(1)} %all-to-all-done.1, f32[4,10,128]{2,1,0:T(8,128)S(1)} %fusion.13, bf16[4,10,5120]{2,1,0:T(8,128)(2,1)S(1)} %all_to_all.69, bf16[1,128,5120]{2,1,0:T(8,128)(2,1)S(1)} %copy-done, f32[4,10]{1,0:T(4,128)S(1)} %bitcast.108), kind=kOutput, calls=%fused_computation.5 | convolution fusion | flops 105533440 | bytes 3461280 | tf_op jit(solution)/shard_map/scd,sch->dh/dot_general | solution.py:98
  236.7 4.3 %reduce-scatter.5.cloned.1.call-done = bf16[1,128,2560]{2,1,0:T(8,128)(2,1)} async-done(((bf16[1,128,5120]{2,1,0:T(8,128)(2,1)}), bf16[1,128,2560]{2,1,0:T(8,128)(2,1)}) %reduce-scatter.5.cloned.1.call-update) | async-done | bytes 655376 | tf_op jit(solution)/shard_map/reduce_scatter | solution.py:105
  241.0 12.8 %reduce-scatter.3.cloned.1.call-done = bf16[1,2560,128]{2,1,0:T(8,128)(2,1)} async-done(((bf16[1,5120,128]{2,1,0:T(8,128)(2,1)}), bf16[1,2560,128]{2,1,0:T(8,128)(2,1)}) %reduce-scatter.3.cloned.1.call-update) | async-done | bytes 655376 | tf_op jit(solution)/shard_map/reduce_scatter | solution.py:102
  (18 shorter events, 0.2 us)
Async XLA Ops:
  7.2 118.3 %copy-start = (bf16[1,128,5120]{2,1,0:T(8,128)(2,1)S(1)}, bf16[1,128,5120]{2,1,0:T(8,128)(2,1)}, u32[]{:S(2)}) copy-start(bf16[1,128,5120]{2,1,0:T(8,128)(2,1)} %param.15) | copy-start | bytes 3932164
  7.2 115.9 %all-reduce.3.cloned.1.call-start = ((), (), s32[]{:S(2)}) async-start(), calls=%async_computation.8 | async-start | bytes 4194304 | tf_op jit(solution)/shard_map/psum | solution.py:32
  14.2 6.9 %copy-start.4 = (s32[128,1]{0,1:T(1,128)S(1)}, s32[128,1]{0,1:T(1,128)}, u32[]{:S(2)}) copy-start(s32[128,1]{0,1:T(1,128)} %param.16) | copy-start | bytes 1540
  14.2 8.1 %copy-start.5 = (s32[8]{0:T(128)S(1)}, s32[8]{0:T(128)}, u32[]{:S(2)}) copy-start(s32[8]{0:T(128)} %param.17) | copy-start | bytes 100
  14.3 25.9 %all-to-all-start = ((bf16[4,32,1280]{2,1,0:T(8,128)(2,1)}), bf16[4,32,1280]{2,1,0:T(8,128)(2,1)S(1)}, u32[]{:S(2)}, u32[]{:S(2)}) async-start(bf16[4,32,1280]{2,1,0:T(8,128)(2,1)} %bitcast.5), calls=%async_computation | async-start | bytes 655360 | tf_op jit(solution)/shard_map/all_to_all | solution.py:59
  40.7 35.3 %copy-start.1 = (bf16[1,5120,128]{2,1,0:T(8,128)(2,1)S(1)}, bf16[1,5120,128]{2,1,0:T(8,128)(2,1)}, u32[]{:S(2)}) copy-start(bf16[1,5120,128]{2,1,0:T(8,128)(2,1)} %param.13) | copy-start | bytes 3932164
  40.7 35.3 %copy-start.3 = (f32[1,128]{1,0:T(1,128)S(1)}, f32[1,128]{1,0:T(1,128)}, u32[]{:S(2)}) copy-start(f32[1,128]{1,0:T(1,128)} %param.14) | copy-start | bytes 1540
  41.9 34.1 %all-to-all-start.1 = ((bf16[4,10,5120]{2,1,0:T(8,128)(2,1)}), bf16[4,10,5120]{2,1,0:T(8,128)(2,1)S(1)}, u32[]{:S(2)}, u32[]{:S(2)}) async-start(bf16[4,10,5120]{2,1,0:T(8,128)(2,1)} %convolution_convert_fusion.2), calls=%async_computation.1 | async-start | bytes 1310720 | tf_op jit(solution)/shard_map/all_to_all | solution.py:63
  45.3 77.8 %copy-start.2 = (f32[4096]{0:T(1024)S(1)}, f32[4096]{0:T(1024)}, u32[]{:S(2)}) copy-start(f32[4096]{0:T(1024)} %param.11) | copy-start | bytes 49156
  45.4 150.2 %all-reduce.5.cloned.1.call-start = ((), (), s32[]{:S(2)}) async-start(), calls=%async_computation.9 | async-start | bytes 1310720 | tf_op jit(solution)/shard_map/psum | solution.py:85
  164.9 76.2 %reduce-scatter.5.cloned.1.call-start = ((), (), s32[]{:S(2)}) async-start(), calls=%async_computation.11 | async-start | bytes 1966080 | tf_op jit(solution)/shard_map/reduce_scatter | solution.py:105
  233.9 19.8 %reduce-scatter.3.cloned.1.call-start = ((), (), s32[]{:S(2)}) async-start(), calls=%async_computation.10 | async-start | bytes 1966080 | tf_op jit(solution)/shard_map/reduce_scatter | solution.py:102
Sparse Core Ops, SparseCore 0:
  14.4 108.6 all-reduce.2
  165.0 30.4 all-reduce.4
  234.0 6.9 reduce-scatter.4
  243.8 9.9 reduce-scatter.2
where the time goes:
time: 261 us; the launch traced here: 260 us
  waiting for transfers between devices  142 us (54%)
  blocking collectives  66 us (25%)
  matrix products  21 us (8%)
  between operations  13.9 us (5%)
  starting transfers between devices  9.97 us (4%)
  other arithmetic  4.94 us (2%)
    psum x1, waiting for transfers between devices, body(): parent_linear = lax.psum(partial_value, 'expert') + parent_bias  46.8 us
    psum x1, waiting for transfers between devices, body(): total_sum = lax.psum(total_part, 'parent')  30.6 us
    all_to_all x1, waiting for transfers between devices, send_slots(): lax.all_to_all(packed, 'expert', split_axis=0, concat_axis=0, tiled=True)  30.3 us
    all_to_all x1, blocking collectives, body(): lax.all_to_all(child_output, 'expert', split_axis=0, concat_axis=0, tiled...  20 us
    all_to_all x1, blocking collectives, send_slots(): lax.all_to_all(packed, 'expert', split_axis=0, concat_axis=0, tiled=True)  19.1 us
    all_to_all x1, waiting for transfers between devices, send_slots(): lax.all_to_all(values, 'expert', split_axis=0, concat_axis=1, tiled=True)  17.5 us
    all_to_all x1, blocking collectives, send_slots(): lax.all_to_all(values, 'expert', split_axis=0, concat_axis=1, tiled=True)  14.7 us
    reduce_scatter x1, waiting for transfers between devices, body(): lax.psum_scatter(encoder_grad[None].astype(jnp.bfloat16), 'dp', scatter_d...  12.8 us
  transfers between devices with their start and end apart: 6, of which 6 were waited for; matrix products, arithmetic and copies ran while one was open for 3% of the time, Pallas kernels for 0%

commit v1 on v0

--- a/solution.py
+++ b/solution.py
@@ -1,6 +1,8 @@
 import jax
 import jax.numpy as jnp
 from jax import lax
+from jax.experimental import pallas as pl
+from jax.experimental.pallas import tpu as pltpu
 from jax.sharding import PartitionSpec as P
 
 CAP = 10
@@ -9,7 +11,7 @@
 ERROR_SCALE = 0.03125
 
 
-def body(
+def general_body(
     activations,
     parent_encoder,
     parent_bias,
@@ -109,6 +111,480 @@
     return (reconstruction, encoder_sum.astype(jnp.bfloat16), decoder_sum.astype(jnp.bfloat16))
 
 
+FUSED_MESH = {"groups": 2, "expert": 4, "parent": 2, "dp": 2}
+OWN = 4
+SLOTS = 48
+TILE = 256
+BF16 = jnp.bfloat16
+F32 = jnp.float32
+
+
+def matmul(left, right, dims=((1,), (0,))):
+    return lax.dot_general(left, right, (dims, ((), ())), preferred_element_type=F32)
+
+
+def fused_kernel(
+    owner_ref,
+    act_ref,
+    w_hbm,
+    bias_ref,
+    wd_hbm,
+    enc_hbm,
+    cbias_ref,
+    dec_hbm,
+    blocks_ref,
+    recon_ref,
+    egrad_ref,
+    dgrad_ref,
+    w_buf,
+    wd_buf,
+    enc,
+    dec,
+    sel,
+    pack,
+    x_slots,
+    e_slots,
+    part_send,
+    part_recv,
+    own_part,
+    gate_send,
+    gate_recv,
+    pa,
+    cl_part,
+    cl_recv,
+    sg_own,
+    sg_recv,
+    c_send,
+    c_recv,
+    acc,
+    tot_send,
+    tot_recv,
+    err,
+    e_pack,
+    ag_part,
+    ag_recv,
+    load_sem,
+    pack_sem,
+    x_recv_sem,
+    e_pack_sem,
+    e_recv_sem,
+    part_send_sem,
+    part_recv_sem,
+    gate_send_sem,
+    gate_recv_sem,
+    pa_send_sem,
+    pa_recv_sem,
+    c_send_sem,
+    c_recv_sem,
+    core_send_sem,
+    core_recv_sem,
+    tot_send_sem,
+    tot_recv_sem,
+):
+    e = lax.axis_index("expert")
+    p = lax.axis_index("parent")
+    d = lax.axis_index("dp")
+    rows, width = act_ref.shape
+    chunk = w_buf.shape[2]
+    home = e // 2
+    side = lax.rem(e, 2)
+
+    def at(o):
+        return lax.rem(e + o, OWN)
+
+    def before(o):
+        return lax.rem(e + OWN - o, OWN)
+
+    loads = []
+    for n, o in enumerate((1, 2, 3, 0)):
+        source = w_hbm.at[:, pl.ds(pl.multiple_of(at(o) * chunk, chunk), chunk)]
+        loads.append(pltpu.make_async_copy(source, w_buf.at[o], load_sem.at[n]))
+    loads.append(pltpu.make_async_copy(enc_hbm.at[0], enc, load_sem.at[4]))
+    loads.append(pltpu.make_async_copy(dec_hbm.at[0], dec, load_sem.at[5]))
+    for o in range(OWN):
+        source = wd_hbm.at[pl.ds(pl.multiple_of(before(o) * chunk, chunk), chunk), :]
+        loads.append(pltpu.make_async_copy(source, wd_buf.at[o], load_sem.at[6 + o]))
+    for load in loads:
+        load.start()
+
+    barrier = pltpu.get_barrier_semaphore()
+    for o in range(OWN):
+        for c in range(2):
+            if o or c:
+                pl.semaphore_signal(
+                    barrier, inc=1, device_id={"expert": at(o), "dp": lax.rem(d + c, 2)}
+                )
+    pl.semaphore_signal(barrier, inc=1, device_id={"parent": 1 - p})
+
+    blocks = blocks_ref[...]
+    hit_rows = []
+    mine = jnp.zeros((1, rows), F32)
+    for o in range(OWN):
+        named = jnp.int32(0)
+        for j in range(OWN):
+            index = p * OWN + j
+            named = named + jnp.where(owner_ref[index] == at(o), index, 0)
+        hit = jnp.max((blocks == named).astype(F32), axis=0, keepdims=True)
+        hit_rows.append(hit)
+    row_id = lax.broadcasted_iota(jnp.int32, (rows, rows), 0)
+    col_id = lax.broadcasted_iota(jnp.int32, (rows, rows), 1)
+    earlier = (row_id < col_id).astype(BF16)
+    slot_id = lax.broadcasted_iota(jnp.int32, (SLOTS, rows), 0).astype(F32)
+    for o in range(OWN):
+        hit8 = jnp.broadcast_to(hit_rows[o], (16, rows))
+        rank = matmul(hit8.astype(BF16), earlier)[0:1]
+        sel[o] = ((slot_id == rank).astype(F32) * hit_rows[o]).astype(BF16)
+
+    pl.semaphore_wait(barrier, 2 * OWN)
+
+    def dispatch(source_ref, pack_ref, slots_ref, send_sems, recv_sems):
+        sends = []
+        for o in (2, 1, 3, 0):
+            pack_ref[o] = matmul(sel[o], source_ref[...]).astype(BF16)
+            copy = pltpu.make_async_remote_copy(
+                src_ref=pack_ref.at[o],
+                dst_ref=slots_ref.at[d, side],
+                send_sem=send_sems.at[o],
+                recv_sem=recv_sems.at[d, side],
+                device_id={"expert": at(o), "dp": home},
+            )
+            if o:
+                copy.start()
+            else:
+
+                @pl.when(home != d)
+                def _():
+                    copy.start()
+
+                @pl.when(home == d)
+                def _():
+                    slots_ref[d, side] = pack_ref[0]
+
+            sends.append(copy)
+        return sends
+
+    def receive_slots(pack_ref, slots_ref, send_sems, recv_sems):
+        for c in range(2):
+            for i in range(2):
+
+                @pl.when(jnp.logical_or(c != d, 2 * d + i != e))
+                def _():
+                    pltpu.make_async_remote_copy(
+                        src_ref=pack_ref.at[0],
+                        dst_ref=slots_ref.at[c, i],
+                        send_sem=send_sems.at[0],
+                        recv_sem=recv_sems.at[c, i],
+                        device_id={"dp": 1 - d},
+                    ).wait_recv()
+
+    def finish_dispatch(sends):
+        for n, copy in enumerate(sends):
+            if n < 3:
+                copy.wait_send()
+            else:
+
+                @pl.when(home != d)
+                def _():
+                    copy.wait_send()
+
+    x_sends = dispatch(act_ref, pack, x_slots, pack_sem, x_recv_sem)
+
+    part_sends = []
+    gates = jnp.zeros((8, rows), F32)
+    gate_row = lax.broadcasted_iota(jnp.int32, (8, rows), 0)
+    for n, o in enumerate((1, 2, 3, 0)):
+        loads[n].wait()
+
+        @pl.loop(0, chunk // TILE)
+        def _(t):
+            columns = pl.ds(pl.multiple_of(t * TILE, TILE), TILE)
+            value = matmul(act_ref[...], w_buf[o, :, columns])
+            if o:
+                part_send[o - 1, :, columns] = value.astype(BF16)
+            else:
+                own_part[:, columns] = value
+
+        if o:
+            copy = pltpu.make_async_remote_copy(
+                src_ref=part_send.at[o - 1],
+                dst_ref=part_recv.at[o - 1],
+                send_sem=part_send_sem.at[o - 1],
+                recv_sem=part_recv_sem.at[o - 1],
+                device_id={"expert": at(o)},
+            )
+            copy.start()
+            part_sends.append(copy)
+        first = matmul(act_ref[...], w_buf[o, :, 0:128])
+        gates = gates + jnp.where(gate_row == at(o), first.T[0:1], 0.0)
+
+    gate_send[...] = gates
+    gate_copies = []
+    for o in (1, 2, 3):
+        copy = pltpu.make_async_remote_copy(
+            src_ref=gate_send,
+            dst_ref=gate_recv.at[o - 1],
+            send_sem=gate_send_sem.at[o - 1],
+            recv_sem=gate_recv_sem.at[o - 1],
+            device_id={"expert": at(o)},
+        )
+        copy.start()
+        gate_copies.append(copy)
+
+    def to_core(source, target, n):
+        return pltpu.make_async_remote_copy(
+            src_ref=source,
+            dst_ref=target,
+            send_sem=core_send_sem.at[n],
+            recv_sem=core_recv_sem.at[n],
+            device_id={"dp": 1 - d},
+        )
+
+    receive_slots(pack, x_slots, pack_sem, x_recv_sem)
+    loads[4].wait()
+    for c in range(2):
+        value = jnp.zeros((SLOTS, enc.shape[1]), F32)
+        for i in range(2):
+            depth = pl.ds(pl.multiple_of((2 * d + i) * width, width), width)
+            value = value + matmul(x_slots[c, i], enc[depth, :])
+        cl_part[c] = value
+    cl_copy = to_core(cl_part, cl_recv, 0)
+    cl_copy.start()
+
+    for copy in gate_copies:
+        copy.wait_recv()
+    sums = gates + gate_recv[0] + gate_recv[1] + gate_recv[2]
+    mine = jnp.zeros((1, rows), F32)
+    for j in range(OWN):
+        gate = jnp.maximum(sums[j : j + 1] + bias_ref[j : j + 1, 0:1], 0.0).astype(BF16)
+        held = jnp.where(owner_ref[p * OWN + j] == e, 1.0, 0.0).astype(F32)
+        mine = mine + gate.astype(F32) * held
+    slot_gate = jnp.sum(sel[0].astype(F32) * mine, axis=1, keepdims=True)
+    sg_own[...] = jnp.broadcast_to(slot_gate, sg_own.shape)
+    sg_copy = to_core(sg_own, sg_recv, 1)
+    sg_copy.start()
+    cl_copy.wait_recv()
+    sg_copy.wait_recv()
+    slot_gates, positives, actives = [], [], []
+    for c in range(2):
+        gate = jnp.where(d == c, sg_own[...], sg_recv[...])
+        positive = jnp.maximum(cl_part[c] + cl_recv[c] + cbias_ref[...], 0.0)
+        slot_gates.append(gate)
+        positives.append(positive)
+        actives.append((positive * positive * gate).astype(BF16))
+    active_here = jnp.where(d == 0, actives[0].astype(F32), actives[1].astype(F32)).astype(BF16)
+    loads[5].wait()
+    c_copies = []
+    for o in (2, 1, 3, 0):
+        columns = pl.ds(pl.multiple_of(at(o) * width, width), width)
+        value = matmul(active_here, dec[:, columns]).astype(BF16)
+        if o:
+            c_send[o - 1] = value
+            copy = pltpu.make_async_remote_copy(
+                src_ref=c_send.at[o - 1],
+                dst_ref=c_recv.at[o],
+                send_sem=c_send_sem.at[o - 1],
+                recv_sem=c_recv_sem.at[o - 1],
+                device_id={"expert": at(o)},
+            )
+            copy.start()
+            c_copies.append(copy)
+        else:
+            c_recv[0] = value
+
+    for copy in part_sends:
+        copy.wait_recv()
+
+    @pl.loop(0, chunk // TILE)
+    def _(t):
+        columns = pl.ds(pl.multiple_of(t * TILE, TILE), TILE)
+        value = own_part[:, columns] + bias_ref[pl.ds(e, 1), columns]
+        for o in range(3):
+            value = value + part_recv[o, :, columns].astype(F32)
+        pa[0, :, columns] = jnp.maximum(value, 0.0).astype(BF16)
+
+    pa_copies = []
+    for o in (1, 2, 3):
+        copy = pltpu.make_async_remote_copy(
+            src_ref=pa.at[0],
+            dst_ref=pa.at[o],
+            send_sem=pa_send_sem.at[o - 1],
+            recv_sem=pa_recv_sem.at[o - 1],
+            device_id={"expert": at(o)},
+        )
+        copy.start()
+        pa_copies.append(copy)
+
+    for o in range(OWN):
+        loads[6 + o].wait()
+        if o:
+            pa_copies[o - 1].wait_recv()
+        if o == OWN - 1:
+            for copy in c_copies:
+                copy.wait_recv()
+
+        @pl.loop(0, width // TILE)
+        def _(t):
+            columns = pl.ds(pl.multiple_of(t * TILE, TILE), TILE)
+            value = matmul(pa[o], wd_buf[o, :, columns])
+            if o:
+                value = value + acc[:, columns]
+            if o == OWN - 1:
+                for q in range(OWN):
+                    value = value + matmul(
+                        sel[(OWN - q) % OWN], c_recv[q, :, columns], ((0,), (0,))
+                    )
+                tot_send[:, columns] = value.astype(BF16)
+            else:
+                acc[:, columns] = value
+
+    tot_copy = pltpu.make_async_remote_copy(
+        src_ref=tot_send,
+        dst_ref=tot_recv,
+        send_sem=tot_send_sem,
+        recv_sem=tot_recv_sem,
+        device_id={"parent": 1 - p},
+    )
+    tot_copy.start()
+    tot_copy.wait_recv()
+
+    @pl.loop(0, width // TILE)
+    def _(t):
+        columns = pl.ds(pl.multiple_of(t * TILE, TILE), TILE)
+        total = tot_send[:, columns].astype(F32) + tot_recv[:, columns].astype(F32)
+        recon_ref[:, columns] = total.astype(BF16)
+        value = (total - act_ref[:, columns].astype(F32)) * ERROR_SCALE
+        err[:, columns] = value.astype(BF16)
+
+    e_sends = dispatch(err, e_pack, e_slots, e_pack_sem, e_recv_sem)
+    receive_slots(e_pack, e_slots, e_pack_sem, e_recv_sem)
+    for c in range(2):
+        value = jnp.zeros((SLOTS, enc.shape[1]), F32)
+        for i in range(2):
+            columns = pl.ds(pl.multiple_of((2 * d + i) * width, width), width)
+            value = value + matmul(e_slots[c, i], dec[:, columns], ((1,), (1,)))
+        ag_part[c] = value
+    ag_copy = to_core(ag_part, ag_recv, 2)
+    ag_copy.start()
+    for i in range(2):
+        for t in range(0, width, TILE):
+            value = jnp.zeros((dgrad_ref.shape[1], TILE), F32)
+            for c in range(2):
+                part = matmul(actives[c], e_slots[c, i, :, t : t + TILE], ((0,), (0,)))
+                value = value + part.astype(BF16).astype(F32)
+            dgrad_ref[0, :, i * width + t : i * width + t + TILE] = value.astype(BF16)
+    ag_copy.wait_recv()
+    linear_grads = []
+    for c in range(2):
+        active_grad = ag_part[c] + ag_recv[c]
+        linear_grads.append((active_grad * slot_gates[c] * 2.0 * positives[c]).astype(BF16))
+    for i in range(2):
+        for t in range(0, width, TILE):
+            value = jnp.zeros((TILE, egrad_ref.shape[2]), F32)
+            for c in range(2):
+                part = matmul(x_slots[c, i, :, t : t + TILE], linear_grads[c], ((0,), (0,)))
+                value = value + part.astype(BF16).astype(F32)
+            egrad_ref[0, i * width + t : i * width + t + TILE, :] = value.astype(BF16)
+
+    finish_dispatch(x_sends)
+    finish_dispatch(e_sends)
+    for copy in part_sends + gate_copies + c_copies + pa_copies:
+        copy.wait_send()
+    for copy in (cl_copy, sg_copy, ag_copy, tot_copy):
+        copy.wait_send()
+
+
+def fused_body(
+    activations,
+    parent_encoder,
+    parent_bias,
+    parent_decoder,
+    child_encoder,
+    child_bias,
+    child_decoder,
+    child_blocks,
+    block_owner,
+):
+    rows, width = activations.shape
+    chunk = parent_encoder.shape[1] // OWN
+    depth, hidden = child_encoder.shape[1:]
+    vmem = pl.BlockSpec(memory_space=pltpu.VMEM)
+    smem = pl.BlockSpec(memory_space=pltpu.SMEM)
+    hbm = pl.BlockSpec(memory_space=pl.ANY)
+    dma = pltpu.SemaphoreType.DMA
+    scratch = [
+        pltpu.VMEM((OWN, width, chunk), BF16),
+        pltpu.VMEM((OWN, chunk, width), BF16),
+        pltpu.VMEM((depth, hidden), BF16),
+        pltpu.VMEM((hidden, depth), BF16),
+        pltpu.VMEM((OWN, SLOTS, rows), BF16),
+        pltpu.VMEM((OWN, SLOTS, width), BF16),
+        pltpu.VMEM((2, 2, SLOTS, width), BF16),
+        pltpu.VMEM((2, 2, SLOTS, width), BF16),
+        pltpu.VMEM((3, rows, chunk), BF16),
+        pltpu.VMEM((3, rows, chunk), BF16),
+        pltpu.VMEM((rows, chunk), F32),
+        pltpu.VMEM((8, rows), F32),
+        pltpu.VMEM((3, 8, rows), F32),
+        pltpu.VMEM((OWN, rows, chunk), BF16),
+        pltpu.VMEM((2, SLOTS, hidden), F32),
+        pltpu.VMEM((2, SLOTS, hidden), F32),
+        pltpu.VMEM((SLOTS, hidden), F32),
+        pltpu.VMEM((SLOTS, hidden), F32),
+        pltpu.VMEM((3, SLOTS, width), BF16),
+        pltpu.VMEM((OWN, SLOTS, width), BF16),
+        pltpu.VMEM((rows, width), F32),
+        pltpu.VMEM((rows, width), BF16),
+        pltpu.VMEM((rows, width), BF16),
+        pltpu.VMEM((rows, width), BF16),
+        pltpu.VMEM((OWN, SLOTS, width), BF16),
+        pltpu.VMEM((2, SLOTS, hidden), F32),
+        pltpu.VMEM((2, SLOTS, hidden), F32),
+        dma((10,)),
+        dma((OWN,)),
+        dma((2, 2)),
+        dma((OWN,)),
+        dma((2, 2)),
+        dma((3,)),
+        dma((3,)),
+        dma((3,)),
+        dma((3,)),
+        dma((3,)),
+        dma((3,)),
+        dma((3,)),
+        dma((3,)),
+        dma((3,)),
+        dma((3,)),
+        dma,
+        dma,
+    ]
+    half = depth // 2
+    return pl.pallas_call(
+        fused_kernel,
+        out_shape=(
+            jax.ShapeDtypeStruct((rows, width), BF16),
+            jax.ShapeDtypeStruct((1, half, hidden), BF16),
+            jax.ShapeDtypeStruct((1, hidden, half), BF16),
+        ),
+        in_specs=[smem, vmem, hbm, vmem, hbm, hbm, vmem, hbm, vmem],
+        out_specs=(vmem, vmem, vmem),
+        scratch_shapes=scratch,
+        compiler_params=pltpu.CompilerParams(
+            collective_id=0, has_side_effects=True, vmem_limit_bytes=52 * 2**20
+        ),
+        name="fused_step",
+    )(
+        block_owner,
+        activations,
+        parent_encoder,
+        parent_bias.reshape(OWN, chunk),
+        parent_decoder,
+        child_encoder,
+        child_bias,
+        child_decoder,
+        child_blocks.T,
+    )
+
+
 def solution(mesh):
     in_specs = (
         P(("groups", "dp"), "expert"),
@@ -126,4 +602,6 @@
         P(("groups", "expert", "parent"), "dp", None),
         P(("groups", "expert", "parent"), None, "dp"),
     )
+    fused = all(mesh.shape[name] == size for name, size in FUSED_MESH.items())
+    body = fused_body if fused else general_body
     return jax.shard_map(body, mesh=mesh, in_specs=in_specs, out_specs=out_specs, check_vma=False)

time: 261 us -> 108 us (0.41)
  waiting for transfers between devices: 142 us -> 0 us
  Pallas kernels: 0 us -> 101 us
  blocking collectives: 66 us -> 0 us
  matrix products: 21 us -> 0 us
  between operations: 13.9 us -> 0.64 us
  starting transfers between devices: 9.97 us -> 0 us
  other arithmetic: 4.94 us -> 0 us
  local copies, waits for them, and re-layouts: 2.16 us -> 6.06 us
    pallas_call x0 -> x1, Pallas kernels: none -> 101 us  [fused_body(): pl.pallas_call(fused_kernel, out_shape=(jax.ShapeDtypeStruct((rows, width...]
    psum x2 -> x0, waiting for transfers between devices: 77.4 us -> none  [the longest x1 46.8 us: body(): parent_linear = lax.psum(partial_value, 'expert') + parent_bias]
    all_to_all x4 -> x0, blocking collectives: 66 us -> none  [the longest x1 20 us: body(): lax.all_to_all(child_output, 'expert', split_axis=0, concat_axis=0, tiled...]
    all_to_all x2 -> x0, waiting for transfers between devices: 47.8 us -> none  [the longest x1 30.3 us: send_slots(): lax.all_to_all(packed, 'expert', split_axis=0, concat_axis=0, tiled=True)]
    dot_general x13 -> x0, matrix products: 21 us -> none  [the longest x1 7.02 us: body(): jnp.dot(activations, parent_encoder, preferred_element_type=jnp.float32)]
    reduce_scatter x2 -> x0, waiting for transfers between devices: 17.1 us -> none  [the longest x1 12.8 us: body(): lax.psum_scatter(encoder_grad[None].astype(jnp.bfloat16), 'dp', scatter_d...]
    all_to_all x2 -> x0, starting transfers between devices: 9.81 us -> none  [the longest x1 6.33 us: send_slots(): lax.all_to_all(values, 'expert', split_axis=0, concat_axis=1, tiled=True)]
    unnamed x13 -> x11, local copies, waits for them, and re-layouts: 0.55 us -> 5.33 us
  transfers between devices with their start and end apart: 6 -> 0, of which waited for: 6 -> 0; matrix products, arithmetic and copies ran while one was open for 3% -> 0% of each run, Pallas kernels for 0% -> 0%
where the time goes in v1:
time: 108 us; the launch traced here: 107 us
  Pallas kernels  101 us (94%)
  local copies, waits for them, and re-layouts  6.06 us (6%)
    pallas_call x1, Pallas kernels, fused_body(): pl.pallas_call(fused_kernel, out_shape=(jax.ShapeDtypeStruct((rows, width...  101 us
    unnamed x11, local copies, waits for them, and re-layouts  5.33 us

profile of v1, /device:TPU:0, one launch (start us, length us, event | category | flops | bytes accessed | tf_op | source)
XLA Modules:
  0.0 107.3 jit_solution(8038129693027163495)
XLA Ops:
  0.6 0.7 reshape.9.bias_ref
  1.4 0.0 copy-start
  1.4 1.0 copy-done
  2.3 0.0 copy-start.1
  2.3 0.7 copy-done.1
  3.0 0.0 copy-start.2
  3.0 0.7 copy-done.2
  3.6 0.0 copy-start.3
  3.6 0.7 copy-done.3
  4.3 100.6 %fused_step.1 = (bf16[128,1280]{1,0:T(8,128)(2,1)S(1)}, bf16[1,2560,128]{2,1,0:T(8,128)(2,1)S(1)}, bf16[1,128,2560]{2,1,0:T(8,128)(2,1)S(1)}) custom-call(s32[8]{0:T(128)S(1)} %copy-done.1, bf16[128,1280]{1,0:T(8,128)(2,1)S(1)} %copy-done, bf16[1280,4096]{1,0:T(8,128)(2,1)} %w_hbm.1, f32[4,1024]{1,0:T(4,128)S(1)} %reshape.9.bias_ref, ...), custom_call_target="tpu_custom_call" | custom-call | tf_op jit(solution)/shard_map/fused_step/pallas_call | solution.py:561
  104.9 0.7 copy.15
  105.6 0.8 copy.16
  106.5 0.8 copy.17
Async XLA Ops:
  1.4 1.0 copy-start
  2.3 0.7 copy-start.1
  3.0 0.7 copy-start.2
  3.6 0.7 copy-start.3

commit v2 on v0

--- a/solution.py
+++ b/solution.py
@@ -1,6 +1,8 @@
 import jax
 import jax.numpy as jnp
 from jax import lax
+from jax.experimental import pallas as pl
+from jax.experimental.pallas import tpu as pltpu
 from jax.sharding import PartitionSpec as P
 
 CAP = 10
@@ -9,7 +11,7 @@
 ERROR_SCALE = 0.03125
 
 
-def body(
+def general_body(
     activations,
     parent_encoder,
     parent_bias,
@@ -109,6 +111,593 @@
     return (reconstruction, encoder_sum.astype(jnp.bfloat16), decoder_sum.astype(jnp.bfloat16))
 
 
+FUSED_MESH = {"groups": 2, "expert": 4, "parent": 2, "dp": 2}
+OWN = 4
+SLOTS = 40
+TILE = 256
+LANES = 128
+CHILD_STEP = 6
+BF16 = jnp.bfloat16
+F32 = jnp.float32
+
+
+def matmul(left, right, dims=((1,), (0,))):
+    return lax.dot_general(left, right, (dims, ((), ())), preferred_element_type=F32)
+
+
+def fused_kernel(
+    owner_hbm,
+    act_hbm,
+    w_hbm,
+    bias_hbm,
+    wd_hbm,
+    enc_hbm,
+    cbias_hbm,
+    dec_hbm,
+    blocks_hbm,
+    recon_ref,
+    egrad_ref,
+    dgrad_ref,
+    owner,
+    act,
+    bias,
+    cbias,
+    blocks,
+    gate_w,
+    w_buf,
+    wd_buf,
+    enc,
+    dec,
+    sel,
+    sel_all,
+    pack,
+    x_slots,
+    e_pack,
+    e_slots,
+    part,
+    rs_send,
+    rs_recv,
+    pa,
+    gate_send,
+    gate_recv,
+    cl_part,
+    cl_recv,
+    sg_own,
+    sg_recv,
+    c_send,
+    c_recv,
+    acc,
+    tot_send,
+    tot_recv,
+    ag_part,
+    ag_recv,
+    small_sem,
+    gate_load_sem,
+    w_sem,
+    wd_sem,
+    pack_sem,
+    x_recv_sem,
+    e_pack_sem,
+    e_recv_sem,
+    rs_send_sem,
+    rs_recv_sem,
+    pa_send_sem,
+    pa_recv_sem,
+    gate_send_sem,
+    gate_recv_sem,
+    c_send_sem,
+    c_recv_sem,
+    core_send_sem,
+    core_recv_sem,
+    tot_send_sem,
+    tot_recv_sem,
+):
+    e = lax.axis_index("expert")
+    p = lax.axis_index("parent")
+    d = lax.axis_index("dp")
+    rows, width = act.shape
+    tiles = w_buf.shape[0]
+    half = tiles // 2
+    col_tiles = width // TILE
+    home = e // 2
+    side = lax.rem(e, 2)
+    last = OWN - 1
+
+    def at(o):
+        return lax.rem(e + o, OWN)
+
+    small = [
+        pltpu.make_async_copy(act_hbm, act, small_sem.at[0]),
+        pltpu.make_async_copy(blocks_hbm, blocks, small_sem.at[1]),
+        pltpu.make_async_copy(owner_hbm, owner, small_sem.at[2]),
+        pltpu.make_async_copy(cbias_hbm, cbias, small_sem.at[3]),
+    ]
+    for n in range(tiles):
+        source = bias_hbm.at[pl.ds(n * TILE, TILE)]
+        small.append(pltpu.make_async_copy(source, bias.at[n, 0], small_sem.at[4 + n]))
+    stride = tiles * TILE // OWN
+    gate_loads = [
+        pltpu.make_async_copy(
+            w_hbm.at[:, pl.ds(j * stride, LANES)], gate_w.at[j], gate_load_sem.at[j]
+        )
+        for j in range(OWN)
+    ]
+    enc_load = pltpu.make_async_copy(enc_hbm.at[0], enc, small_sem.at[4 + tiles])
+    dec_load = pltpu.make_async_copy(dec_hbm.at[0], dec, small_sem.at[5 + tiles])
+
+    def w_load(g):
+        source = w_hbm.at[:, pl.ds(pl.multiple_of(g * TILE, TILE), TILE)]
+        return pltpu.make_async_copy(source, w_buf.at[g], w_sem.at[g])
+
+    def wd_load(g):
+        source = wd_hbm.at[pl.ds(pl.multiple_of(g * TILE, TILE), TILE), :]
+        return pltpu.make_async_copy(source, wd_buf.at[g], wd_sem.at[g])
+
+    for load in small + gate_loads:
+        load.start()
+
+    @pl.loop(0, half + last)
+    def _(s):
+        up, down = s - e, s - last + e
+
+        @pl.when(jnp.logical_and(up >= 0, up < half))
+        def _():
+            w_load(half + up).start()
+
+        @pl.when(jnp.logical_and(down >= 0, down < half))
+        def _():
+            w_load(down).start()
+
+    enc_load.start()
+    dec_load.start()
+    for t in range(half):
+        wd_load(t).start()
+        wd_load(half + t).start()
+
+    barrier = pltpu.get_barrier_semaphore()
+    for o in range(OWN):
+        for c in range(2):
+            if o or c:
+                pl.semaphore_signal(
+                    barrier, inc=1, device_id={"expert": at(o), "dp": lax.rem(d + c, 2)}
+                )
+    pl.semaphore_signal(barrier, inc=1, device_id={"parent": 1 - p})
+    acc[...] = jnp.zeros_like(acc)
+    for load in small:
+        load.wait()
+
+    named_blocks = blocks[...]
+    row_id = lax.broadcasted_iota(jnp.int32, (rows, rows), 0)
+    col_id = lax.broadcasted_iota(jnp.int32, (rows, rows), 1)
+    earlier = (row_id < col_id).astype(BF16)
+    slot_id = lax.broadcasted_iota(jnp.int32, (SLOTS, rows), 0).astype(F32)
+    picks = []
+    for o in range(OWN):
+        named = jnp.int32(0)
+        for j in range(OWN):
+            index = p * OWN + j
+            named = named + jnp.where(owner[index] == at(o), index, 0)
+        hit = jnp.max((named_blocks == named).astype(F32), axis=0, keepdims=True)
+        rank = matmul(jnp.broadcast_to(hit, (16, rows)).astype(BF16), earlier)[0:1]
+        pick = (slot_id == rank).astype(F32) * hit
+        picks.append(pick)
+        sel[o] = pick.astype(BF16)
+    sel_all[...] = jnp.concatenate([picks[(OWN - q) % OWN] for q in range(OWN)], 0).astype(BF16)
+
+    gates = jnp.zeros((8, rows), F32)
+    gate_row = lax.broadcasted_iota(jnp.int32, (8, rows), 0)
+    for j in range(OWN):
+        gate_loads[j].wait()
+        first = matmul(act[...], gate_w[j])
+        gates = gates + jnp.where(gate_row == j, first.T[0:1], 0.0)
+    gate_send[...] = gates
+
+    pl.semaphore_wait(barrier, 2 * OWN)
+
+    gate_copies = []
+    for o in (1, 2, 3):
+        copy = pltpu.make_async_remote_copy(
+            src_ref=gate_send,
+            dst_ref=gate_recv.at[o - 1],
+            send_sem=gate_send_sem.at[o - 1],
+            recv_sem=gate_recv_sem.at[o - 1],
+            device_id={"expert": at(o)},
+        )
+        copy.start()
+        gate_copies.append(copy)
+
+    def put(ref, value):
+        ref[0:SLOTS, :] = value[:, 0:LANES]
+        ref[SLOTS : 2 * SLOTS, :] = value[:, LANES : 2 * LANES]
+
+    def slot_copy(o, pack_ref, slots_ref, send_sem, recv_sem):
+        return pltpu.make_async_remote_copy(
+            src_ref=pack_ref,
+            dst_ref=slots_ref,
+            send_sem=send_sem,
+            recv_sem=recv_sem,
+            device_id={"expert": at(o), "dp": home},
+        )
+
+    def unless_local(o, action):
+        if o:
+            action()
+        else:
+            pl.when(home != d)(action)
+
+    def is_remote(c, i):
+        return jnp.logical_or(c != d, 2 * d + i != e)
+
+    def gather(ref, c, i):
+        pieces = []
+        for t in range(col_tiles):
+            pieces.append(ref[c, i, t, 0:SLOTS, :].astype(F32))
+            pieces.append(ref[c, i, t, SLOTS : 2 * SLOTS, :].astype(F32))
+        return jnp.concatenate(pieces, axis=1)
+
+    x_sends = []
+    for o in (2, 1, 3, 0):
+        for t in range(col_tiles):
+            value = matmul(sel[o], act[:, t * TILE : (t + 1) * TILE]).astype(BF16)
+            put(pack.at[o, t], value)
+        copy = slot_copy(
+            o, pack.at[o], x_slots.at[d, side], pack_sem.at[o], x_recv_sem.at[d, side]
+        )
+        unless_local(o, copy.start)
+        x_sends.append((o, copy))
+
+    @pl.when(home == d)
+    def _():
+        x_slots[d, side] = pack[0]
+
+    def neighbour(g, move, source, target, send_sems, recv_sems):
+        return pltpu.make_async_remote_copy(
+            src_ref=source.at[g],
+            dst_ref=target.at[g],
+            send_sem=send_sems.at[g],
+            recv_sem=recv_sems.at[g],
+            device_id={"expert": jnp.clip(e + move, 0, last)},
+        )
+
+    def rs_copy(g, move):
+        return neighbour(g, move, rs_send, rs_recv, rs_send_sem, rs_recv_sem)
+
+    def pa_copy(g, move):
+        return neighbour(g, move, pa, pa, pa_send_sem, pa_recv_sem)
+
+    def reduce_tile(g, move, first, end):
+        w_load(g).wait()
+        part[...] = matmul(act[...], w_buf[g])
+
+        @pl.when(e == first)
+        def _():
+            rs_send[g] = part[...].astype(BF16)
+
+        @pl.when(e != first)
+        def _():
+            rs_copy(g, move).wait_recv()
+            value = part[...] + rs_recv[g].astype(F32)
+
+            @pl.when(e != end)
+            def _():
+                rs_send[g] = value.astype(BF16)
+
+            @pl.when(e == end)
+            def _():
+                pa[g] = jnp.maximum(value + bias[g], 0.0).astype(BF16)
+
+        @pl.when(e != end)
+        def _():
+            rs_copy(g, move).start()
+
+    def spread_tile(g, move, first, end):
+        @pl.when(e != first)
+        def _():
+            pa_copy(g, move).wait_recv()
+
+        @pl.when(e != end)
+        def _():
+            pa_copy(g, move).start()
+
+        wd_load(g).wait()
+        acc[...] += matmul(pa[g], wd_buf[g])
+
+    def within(t):
+        return jnp.logical_and(t >= 0, t < half)
+
+    def step(s):
+        @pl.when(within(s - e))
+        def _():
+            reduce_tile(half + s - e, 1, 0, last)
+
+        @pl.when(within(s - last + e))
+        def _():
+            reduce_tile(s - last + e, -1, last, 0)
+
+        @pl.when(within(s - last - e))
+        def _():
+            spread_tile(s - last - e, 1, 0, last)
+
+        @pl.when(within(s - 2 * last + e))
+        def _():
+            spread_tile(half + s - 2 * last + e, -1, last, 0)
+
+    def to_core(source, target, n):
+        return pltpu.make_async_remote_copy(
+            src_ref=source,
+            dst_ref=target,
+            send_sem=core_send_sem.at[n],
+            recv_sem=core_recv_sem.at[n],
+            device_id={"dp": 1 - d},
+        )
+
+    pl.loop(0, CHILD_STEP)(step)
+
+    for c in range(2):
+        for i in range(2):
+
+            @pl.when(is_remote(c, i))
+            def _():
+                slot_copy(
+                    1, pack.at[1], x_slots.at[c, i], pack_sem.at[1], x_recv_sem.at[c, i]
+                ).wait_recv()
+
+    enc_load.wait()
+    inputs = []
+    value = jnp.zeros((2 * SLOTS, enc.shape[1]), F32)
+    for i in range(2):
+        depth = pl.ds(pl.multiple_of((2 * d + i) * width, width), width)
+        rows_in = jnp.concatenate([gather(x_slots, c, i) for c in range(2)], 0).astype(BF16)
+        value = value + matmul(rows_in, enc[depth, :])
+    cl_part[...] = value
+    cl_copy = to_core(cl_part, cl_recv, 0)
+    cl_copy.start()
+    for copy in gate_copies:
+        copy.wait_recv()
+    sums = gate_send[...] + gate_recv[0] + gate_recv[1] + gate_recv[2]
+    mine = jnp.zeros((1, rows), F32)
+    for j in range(OWN):
+        gate_bias = bias[j * tiles // OWN][:, 0:1]
+        gate = jnp.maximum(sums[j : j + 1] + gate_bias, 0.0).astype(BF16)
+        held = jnp.where(owner[p * OWN + j] == e, 1.0, 0.0).astype(F32)
+        mine = mine + gate.astype(F32) * held
+    slot_gate = jnp.sum(sel[0].astype(F32) * mine, axis=1, keepdims=True)
+    sg_own[...] = jnp.broadcast_to(slot_gate, sg_own.shape)
+    sg_copy = to_core(sg_own, sg_recv, 1)
+    sg_copy.start()
+
+    pl.loop(CHILD_STEP, CHILD_STEP + 1)(step)
+
+    cl_copy.wait_recv()
+    sg_copy.wait_recv()
+    own_gate, other_gate = sg_own[...], sg_recv[...]
+    slot_gates = jnp.concatenate(
+        [jnp.where(d == 0, own_gate, other_gate), jnp.where(d == 0, other_gate, own_gate)], 0
+    )
+    positive = jnp.maximum(cl_part[...] + cl_recv[...] + cbias[...], 0.0)
+    active = positive * positive * slot_gates
+    active_here = jnp.where(d == 0, active[0:SLOTS], active[SLOTS : 2 * SLOTS]).astype(BF16)
+    active = active.astype(BF16)
+    dec_load.wait()
+    c_copies = []
+    for o in (2, 1, 3, 0):
+        for t in range(col_tiles):
+            columns = pl.ds(pl.multiple_of(at(o) * width + t * TILE, TILE), TILE)
+            value = matmul(active_here, dec[:, columns]).astype(BF16)
+            put(c_send.at[o - 1, t] if o else c_recv.at[0, t], value)
+        if o:
+            copy = pltpu.make_async_remote_copy(
+                src_ref=c_send.at[o - 1],
+                dst_ref=c_recv.at[o],
+                send_sem=c_send_sem.at[o - 1],
+                recv_sem=c_recv_sem.at[o - 1],
+                device_id={"expert": at(o)},
+            )
+            copy.start()
+            c_copies.append(copy)
+
+    pl.loop(CHILD_STEP + 1, half + 2 * last)(step)
+
+    for copy in c_copies:
+        copy.wait_recv()
+    tot_copies = []
+    for t in range(col_tiles):
+        halves = []
+        for h in range(2):
+            pieces = [
+                c_recv[q, t, h * SLOTS : (h + 1) * SLOTS, :].astype(F32) for q in range(OWN)
+            ]
+            halves.append(jnp.concatenate(pieces, 0))
+        outputs = jnp.concatenate(halves, axis=1).astype(BF16)
+        value = acc[:, t * TILE : (t + 1) * TILE] + matmul(sel_all[...], outputs, ((0,), (0,)))
+        tot_send[t] = value.astype(BF16)
+        copy = pltpu.make_async_remote_copy(
+            src_ref=tot_send.at[t],
+            dst_ref=tot_recv.at[t],
+            send_sem=tot_send_sem.at[t],
+            recv_sem=tot_recv_sem.at[t],
+            device_id={"parent": 1 - p},
+        )
+        copy.start()
+        tot_copies.append(copy)
+    e_sends = []
+    for t in range(col_tiles):
+        columns = slice(t * TILE, (t + 1) * TILE)
+        tot_copies[t].wait_recv()
+        total = tot_send[t].astype(F32) + tot_recv[t].astype(F32)
+        recon_ref[:, columns] = total.astype(BF16)
+        value = (total - act[:, columns].astype(F32)) * ERROR_SCALE
+        error = value.astype(BF16)
+        for o in (2, 1, 3, 0):
+            put(e_pack.at[o, t], matmul(sel[o], error).astype(BF16))
+            copy = slot_copy(
+                o,
+                e_pack.at[o, t],
+                e_slots.at[d, side, t],
+                e_pack_sem.at[o, t],
+                e_recv_sem.at[d, side, t],
+            )
+            unless_local(o, copy.start)
+            e_sends.append((o, copy))
+
+    @pl.when(home == d)
+    def _():
+        e_slots[d, side] = e_pack[0]
+
+    for t in range(col_tiles):
+        for c in range(2):
+            for i in range(2):
+
+                @pl.when(is_remote(c, i))
+                def _():
+                    slot_copy(
+                        1,
+                        e_pack.at[1, t],
+                        e_slots.at[c, i, t],
+                        e_pack_sem.at[1, t],
+                        e_recv_sem.at[c, i, t],
+                    ).wait_recv()
+
+    errors = []
+    value = jnp.zeros((2 * SLOTS, enc.shape[1]), F32)
+    for i in range(2):
+        columns = pl.ds(pl.multiple_of((2 * d + i) * width, width), width)
+        errors.append(jnp.concatenate([gather(e_slots, c, i) for c in range(2)], 0).astype(BF16))
+        value = value + matmul(errors[i], dec[:, columns], ((1,), (1,)))
+    ag_part[...] = value
+    ag_copy = to_core(ag_part, ag_recv, 2)
+    ag_copy.start()
+    for i in range(2):
+        value = matmul(active, errors[i], ((0,), (0,)))
+        dgrad_ref[0, :, i * width : (i + 1) * width] = value.astype(BF16)
+    ag_copy.wait_recv()
+    active_grad = ag_part[...] + ag_recv[...]
+    linear_grad = (active_grad * slot_gates * 2.0 * positive).astype(BF16)
+    for i in range(2):
+        rows_in = jnp.concatenate([gather(x_slots, c, i) for c in range(2)], 0).astype(BF16)
+        value = matmul(rows_in, linear_grad, ((0,), (0,)))
+        egrad_ref[0, i * width : (i + 1) * width, :] = value.astype(BF16)
+
+    for o, copy in x_sends + e_sends:
+        unless_local(o, copy.wait_send)
+    for copy in gate_copies + c_copies + tot_copies + [cl_copy, sg_copy, ag_copy]:
+        copy.wait_send()
+
+    @pl.loop(0, half)
+    def _(t):
+        @pl.when(e != 0)
+        def _():
+            rs_copy(t, -1).wait_send()
+            pa_copy(half + t, -1).wait_send()
+
+        @pl.when(e != last)
+        def _():
+            rs_copy(half + t, 1).wait_send()
+            pa_copy(t, 1).wait_send()
+
+
+def fused_body(
+    activations,
+    parent_encoder,
+    parent_bias,
+    parent_decoder,
+    child_encoder,
+    child_bias,
+    child_decoder,
+    child_blocks,
+    block_owner,
+):
+    rows, width = activations.shape
+    tiles = parent_encoder.shape[1] // TILE
+    cols = width // TILE
+    depth, hidden = child_encoder.shape[1:]
+    vmem = pl.BlockSpec(memory_space=pltpu.VMEM)
+    hbm = pl.BlockSpec(memory_space=pl.ANY)
+    dma = pltpu.SemaphoreType.DMA
+    slots = (cols, 2 * SLOTS, LANES)
+    scratch = [
+        pltpu.SMEM(block_owner.shape, jnp.int32),
+        pltpu.VMEM((rows, width), BF16),
+        pltpu.VMEM((tiles, 1, TILE), F32),
+        pltpu.VMEM(child_bias.shape, F32),
+        pltpu.VMEM(child_blocks.shape[::-1], jnp.int32),
+        pltpu.VMEM((OWN, width, LANES), BF16),
+        pltpu.VMEM((tiles, width, TILE), BF16),
+        pltpu.VMEM((tiles, TILE, width), BF16),
+        pltpu.VMEM((depth, hidden), BF16),
+        pltpu.VMEM((hidden, depth), BF16),
+        pltpu.VMEM((OWN, SLOTS, rows), BF16),
+        pltpu.VMEM((OWN * SLOTS, rows), BF16),
+        pltpu.VMEM((OWN,) + slots, BF16),
+        pltpu.VMEM((2, 2) + slots, BF16),
+        pltpu.VMEM((OWN,) + slots, BF16),
+        pltpu.VMEM((2, 2) + slots, BF16),
+        pltpu.VMEM((rows, TILE), F32),
+        pltpu.VMEM((tiles, rows, TILE), BF16),
+        pltpu.VMEM((tiles, rows, TILE), BF16),
+        pltpu.VMEM((tiles, rows, TILE), BF16),
+        pltpu.VMEM((8, rows), F32),
+        pltpu.VMEM((3, 8, rows), F32),
+        pltpu.VMEM((2 * SLOTS, hidden), F32),
+        pltpu.VMEM((2 * SLOTS, hidden), F32),
+        pltpu.VMEM((SLOTS, hidden), F32),
+        pltpu.VMEM((SLOTS, hidden), F32),
+        pltpu.VMEM((3,) + slots, BF16),
+        pltpu.VMEM((OWN,) + slots, BF16),
+        pltpu.VMEM((rows, width), F32),
+        pltpu.VMEM((cols, rows, TILE), BF16),
+        pltpu.VMEM((cols, rows, TILE), BF16),
+        pltpu.VMEM((2 * SLOTS, hidden), F32),
+        pltpu.VMEM((2 * SLOTS, hidden), F32),
+        dma((6 + tiles,)),
+        dma((OWN,)),
+        dma((tiles,)),
+        dma((tiles,)),
+        dma((OWN,)),
+        dma((2, 2)),
+        dma((OWN, cols)),
+        dma((2, 2, cols)),
+        dma((tiles,)),
+        dma((tiles,)),
+        dma((tiles,)),
+        dma((tiles,)),
+        dma((3,)),
+        dma((3,)),
+        dma((3,)),
+        dma((3,)),
+        dma((3,)),
+        dma((3,)),
+        dma((cols,)),
+        dma((cols,)),
+    ]
+    half = depth // 2
+    return pl.pallas_call(
+        fused_kernel,
+        out_shape=(
+            jax.ShapeDtypeStruct((rows, width), BF16),
+            jax.ShapeDtypeStruct((1, half, hidden), BF16),
+            jax.ShapeDtypeStruct((1, hidden, half), BF16),
+        ),
+        in_specs=[hbm] * 9,
+        out_specs=(vmem, vmem, vmem),
+        scratch_shapes=scratch,
+        compiler_params=pltpu.CompilerParams(
+            collective_id=0, has_side_effects=True, vmem_limit_bytes=52 * 2**20
+        ),
+        name="fused_step",
+    )(
+        block_owner,
+        activations,
+        parent_encoder,
+        parent_bias,
+        parent_decoder,
+        child_encoder,
+        child_bias,
+        child_decoder,
+        child_blocks.T,
+    )
+
+
 def solution(mesh):
     in_specs = (
         P(("groups", "dp"), "expert"),
@@ -126,4 +715,6 @@
         P(("groups", "expert", "parent"), "dp", None),
         P(("groups", "expert", "parent"), None, "dp"),
     )
+    fused = all(mesh.shape[name] == size for name, size in FUSED_MESH.items())
+    body = fused_body if fused else general_body
     return jax.shard_map(body, mesh=mesh, in_specs=in_specs, out_specs=out_specs, check_vma=False)

time: 261 us -> 87.6 us (0.34)
  waiting for transfers between devices: 142 us -> 0 us
  Pallas kernels: 0 us -> 80.7 us
  blocking collectives: 66 us -> 0 us
  matrix products: 21 us -> 0 us
  between operations: 13.9 us -> 0.66 us
  starting transfers between devices: 9.97 us -> 0 us
  other arithmetic: 4.94 us -> 0 us
  local copies, waits for them, and re-layouts: 2.16 us -> 6.05 us
    pallas_call x0 -> x1, Pallas kernels: none -> 80.7 us  [fused_body(): pl.pallas_call(fused_kernel, out_shape=(jax.ShapeDtypeStruct((rows, width...]
    psum x2 -> x0, waiting for transfers between devices: 77.4 us -> none  [the longest x1 46.8 us: body(): parent_linear = lax.psum(partial_value, 'expert') + parent_bias]
    all_to_all x4 -> x0, blocking collectives: 66 us -> none  [the longest x1 20 us: body(): lax.all_to_all(child_output, 'expert', split_axis=0, concat_axis=0, tiled...]
    all_to_all x2 -> x0, waiting for transfers between devices: 47.8 us -> none  [the longest x1 30.3 us: send_slots(): lax.all_to_all(packed, 'expert', split_axis=0, concat_axis=0, tiled=True)]
    dot_general x13 -> x0, matrix products: 21 us -> none  [the longest x1 7.02 us: body(): jnp.dot(activations, parent_encoder, preferred_element_type=jnp.float32)]
    reduce_scatter x2 -> x0, waiting for transfers between devices: 17.1 us -> none  [the longest x1 12.8 us: body(): lax.psum_scatter(encoder_grad[None].astype(jnp.bfloat16), 'dp', scatter_d...]
    all_to_all x2 -> x0, starting transfers between devices: 9.81 us -> none  [the longest x1 6.33 us: send_slots(): lax.all_to_all(values, 'expert', split_axis=0, concat_axis=1, tiled=True)]
    unnamed x13, local copies, waits for them, and re-layouts: 0.55 us -> 6.05 us
  transfers between devices with their start and end apart: 6 -> 0, of which waited for: 6 -> 0; matrix products, arithmetic and copies ran while one was open for 3% -> 0% of each run, Pallas kernels for 0% -> 0%
where the time goes in v2:
time: 87.6 us; the launch traced here: 87.4 us
  Pallas kernels  80.7 us (92%)
  local copies, waits for them, and re-layouts  6.05 us (7%)
    pallas_call x1, Pallas kernels, fused_body(): pl.pallas_call(fused_kernel, out_shape=(jax.ShapeDtypeStruct((rows, width...  80.7 us
    unnamed x13, local copies, waits for them, and re-layouts  6.05 us

profile of v2, /device:TPU:0, one launch (start us, length us, event | category | flops | bytes accessed | tf_op | source)
XLA Modules:
  0.0 87.4 jit_solution(12194842837949894031)
XLA Ops:
  0.6 0.0 copy-start
  0.6 1.0 %copy-done = bf16[128,1280]{1,0:T(8,128)(2,1)S(1)} copy-done((bf16[128,1280]{1,0:T(8,128)(2,1)S(1)}, bf16[128,1280]{1,0:T(8,128)(2,1)}, u32[]{:S(2)}) %copy-start) | copy-done | bytes 327704
  1.6 0.0 copy-start.1
  1.6 0.7 copy-done.1
  2.3 0.0 copy-start.2
  2.3 0.7 copy-done.2
  3.0 0.0 copy-start.3
  3.0 0.7 copy-done.3
  3.6 0.0 copy-start.4
  3.6 0.7 copy-done.4
  4.3 80.7 %fused_step.1 = (bf16[128,1280]{1,0:T(8,128)(2,1)S(1)}, bf16[1,2560,128]{2,1,0:T(8,128)(2,1)S(1)}, bf16[1,128,2560]{2,1,0:T(8,128)(2,1)S(1)}) custom-call(s32[8]{0:T(128)S(1)} %copy-done.2, bf16[128,1280]{1,0:T(8,128)(2,1)S(1)} %copy-done, bf16[1280,4096]{1,0:T(8,128)(2,1)} %w_hbm.1, f32[4096]{0:T(1024)S(1)} %copy-done.1, bf16[4096,1280]{1,0:T(8,128)(2,1)} %wd_hbm.1, ...), custom_call_target="tpu_custom_call" | custom-call | tf_op jit(solution)/shard_map/fused_step/pallas_call | solution.py:674
  85.0 0.7 copy.15
  85.7 0.8 copy.16
  86.5 0.8 copy.17
Async XLA Ops:
  0.6 1.0 %copy-start = (bf16[128,1280]{1,0:T(8,128)(2,1)S(1)}, bf16[128,1280]{1,0:T(8,128)(2,1)}, u32[]{:S(2)}) copy-start(bf16[128,1280]{1,0:T(8,128)(2,1)} %act_hbm.1) | copy-start | bytes 983044
  1.6 0.7 copy-start.1
  2.3 0.7 copy-start.2
  3.0 0.7 copy-start.3
  3.6 0.7 copy-start.4

commit v3 on v2

--- a/solution.py
+++ b/solution.py
@@ -116,7 +116,9 @@
 SLOTS = 40
 TILE = 256
 LANES = 128
-CHILD_STEP = 6
+SKEW = 2
+DISPATCH_STEP = 2
+CHILD_STEP = 12
 BF16 = jnp.bfloat16
 F32 = jnp.float32
 
@@ -236,9 +238,9 @@
     for load in small + gate_loads:
         load.start()
 
-    @pl.loop(0, half + last)
+    @pl.loop(0, half + SKEW * last)
     def _(s):
-        up, down = s - e, s - last + e
+        up, down = s - SKEW * e, s - SKEW * (last - e)
 
         @pl.when(jnp.logical_and(up >= 0, up < half))
         def _():
@@ -335,6 +337,100 @@
             pieces.append(ref[c, i, t, SLOTS : 2 * SLOTS, :].astype(F32))
         return jnp.concatenate(pieces, axis=1)
 
+    def neighbour(g, move, source, target, send_sems, recv_sems):
+        return pltpu.make_async_remote_copy(
+            src_ref=source.at[g],
+            dst_ref=target.at[g],
+            send_sem=send_sems.at[g],
+            recv_sem=recv_sems.at[g],
+            device_id={"expert": jnp.clip(e + move, 0, last)},
+        )
+
+    def rs_copy(g, move):
+        return neighbour(g, move, rs_send, rs_recv, rs_send_sem, rs_recv_sem)
+
+    def pa_copy(g, move):
+        return neighbour(g, move, pa, pa, pa_send_sem, pa_recv_sem)
+
+    def reduce_tile(g, move, first, end):
+        w_load(g).wait()
+        part[...] = matmul(act[...], w_buf[g])
+
+        @pl.when(e == first)
+        def _():
+            rs_send[g] = part[...].astype(BF16)
+
+        @pl.when(e != first)
+        def _():
+            rs_copy(g, move).wait_recv()
+            value = part[...] + rs_recv[g].astype(F32)
+
+            @pl.when(e != end)
+            def _():
+                rs_send[g] = value.astype(BF16)
+
+            @pl.when(e == end)
+            def _():
+                pa[g] = jnp.maximum(value + bias[g], 0.0).astype(BF16)
+
+        @pl.when(e != end)
+        def _():
+            rs_copy(g, move).start()
+
+    def receive_tile(g, move, first, end):
+        @pl.when(e != first)
+        def _():
+            pa_copy(g, move).wait_recv()
+
+        @pl.when(e != end)
+        def _():
+            pa_copy(g, move).start()
+
+    def use_tile(g):
+        wd_load(g).wait()
+        acc[...] += matmul(pa[g], wd_buf[g])
+
+    def within(t):
+        return jnp.logical_and(t >= 0, t < half)
+
+    def step(s):
+        up, down = s - SKEW * e, s - SKEW * (last - e)
+        back_down, back_up = s - SKEW * (last + e), s - SKEW * (2 * last - e)
+
+        @pl.when(within(up))
+        def _():
+            reduce_tile(half + up, 1, 0, last)
+
+        @pl.when(within(down))
+        def _():
+            reduce_tile(down, -1, last, 0)
+
+        @pl.when(within(back_down))
+        def _():
+            receive_tile(back_down, 1, 0, last)
+
+        @pl.when(within(back_up))
+        def _():
+            receive_tile(half + back_up, -1, last, 0)
+
+        @pl.when(within(back_down))
+        def _():
+            use_tile(back_down)
+
+        @pl.when(within(back_up))
+        def _():
+            use_tile(half + back_up)
+
+    def to_core(source, target, n):
+        return pltpu.make_async_remote_copy(
+            src_ref=source,
+            dst_ref=target,
+            send_sem=core_send_sem.at[n],
+            recv_sem=core_recv_sem.at[n],
+            device_id={"dp": 1 - d},
+        )
+
+    pl.loop(0, DISPATCH_STEP)(step)
     x_sends = []
     for o in (2, 1, 3, 0):
         for t in range(col_tiles):
@@ -350,88 +446,7 @@
     def _():
         x_slots[d, side] = pack[0]
 
-    def neighbour(g, move, source, target, send_sems, recv_sems):
-        return pltpu.make_async_remote_copy(
-            src_ref=source.at[g],
-            dst_ref=target.at[g],
-            send_sem=send_sems.at[g],
-            recv_sem=recv_sems.at[g],
-            device_id={"expert": jnp.clip(e + move, 0, last)},
-        )
-
-    def rs_copy(g, move):
-        return neighbour(g, move, rs_send, rs_recv, rs_send_sem, rs_recv_sem)
-
-    def pa_copy(g, move):
-        return neighbour(g, move, pa, pa, pa_send_sem, pa_recv_sem)
-
-    def reduce_tile(g, move, first, end):
-        w_load(g).wait()
-        part[...] = matmul(act[...], w_buf[g])
-
-        @pl.when(e == first)
-        def _():
-            rs_send[g] = part[...].astype(BF16)
-
-        @pl.when(e != first)
-        def _():
-            rs_copy(g, move).wait_recv()
-            value = part[...] + rs_recv[g].astype(F32)
-
-            @pl.when(e != end)
-            def _():
-                rs_send[g] = value.astype(BF16)
-
-            @pl.when(e == end)
-            def _():
-                pa[g] = jnp.maximum(value + bias[g], 0.0).astype(BF16)
-
-        @pl.when(e != end)
-        def _():
-            rs_copy(g, move).start()
-
-    def spread_tile(g, move, first, end):
-        @pl.when(e != first)
-        def _():
-            pa_copy(g, move).wait_recv()
-
-        @pl.when(e != end)
-        def _():
-            pa_copy(g, move).start()
-
-        wd_load(g).wait()
-        acc[...] += matmul(pa[g], wd_buf[g])
-
-    def within(t):
-        return jnp.logical_and(t >= 0, t < half)
-
-    def step(s):
-        @pl.when(within(s - e))
-        def _():
-            reduce_tile(half + s - e, 1, 0, last)
-
-        @pl.when(within(s - last + e))
-        def _():
-            reduce_tile(s - last + e, -1, last, 0)
-
-        @pl.when(within(s - last - e))
-        def _():
-            spread_tile(s - last - e, 1, 0, last)
-
-        @pl.when(within(s - 2 * last + e))
-        def _():
-            spread_tile(half + s - 2 * last + e, -1, last, 0)
-
-    def to_core(source, target, n):
-        return pltpu.make_async_remote_copy(
-            src_ref=source,
-            dst_ref=target,
-            send_sem=core_send_sem.at[n],
-            recv_sem=core_recv_sem.at[n],
-            device_id={"dp": 1 - d},
-        )
-
-    pl.loop(0, CHILD_STEP)(step)
+    pl.loop(DISPATCH_STEP, CHILD_STEP)(step)
 
     for c in range(2):
         for i in range(2):
@@ -496,7 +511,7 @@
             copy.start()
             c_copies.append(copy)
 
-    pl.loop(CHILD_STEP + 1, half + 2 * last)(step)
+    pl.loop(CHILD_STEP + 1, half + 2 * SKEW * last)(step)
 
     for copy in c_copies:
         copy.wait_recv()
@@ -682,7 +697,7 @@
         out_specs=(vmem, vmem, vmem),
         scratch_shapes=scratch,
         compiler_params=pltpu.CompilerParams(
-            collective_id=0, has_side_effects=True, vmem_limit_bytes=52 * 2**20
+            collective_id=0, has_side_effects=True, vmem_limit_bytes=63 * 2**20
         ),
         name="fused_step",
     )(

time: 87.6 us -> 79.1 us (0.903)
  Pallas kernels: 80.7 us -> 72.6 us
    pallas_call x1, Pallas kernels: 80.7 us -> 72.6 us  [fused_body(): pl.pallas_call(fused_kernel, out_shape=(jax.ShapeDtypeStruct((rows, width...]
    unnamed x13 -> x3, local copies, waits for them, and re-layouts: 6.05 us -> 5.65 us
where the time goes in v3:
time: 79.1 us; the launch traced here: 78.9 us
  Pallas kernels  72.6 us (92%)
  local copies, waits for them, and re-layouts  5.65 us (7%)
    pallas_call x1, Pallas kernels, fused_body(): pl.pallas_call(fused_kernel, out_shape=(jax.ShapeDtypeStruct((rows, width...  72.6 us
    unnamed x3, local copies, waits for them, and re-layouts  5.65 us

profile of v3, /device:TPU:0, one launch (start us, length us, event | category | flops | bytes accessed | tf_op | source)
XLA Modules:
  0.0 78.9 jit_solution(9721040746385933150)
XLA Ops:
  0.6 72.6 %fused_step.1 = (bf16[128,1280]{1,0:T(8,128)(2,1)}, bf16[1,2560,128]{2,1,0:T(8,128)(2,1)}, bf16[1,128,2560]{2,1,0:T(8,128)(2,1)}) custom-call(s32[8]{0:T(128)} %owner_hbm.1, bf16[128,1280]{1,0:T(8,128)(2,1)} %act_hbm.1, bf16[1280,4096]{1,0:T(8,128)(2,1)} %w_hbm.1, f32[4096]{0:T(1024)} %bias_hbm.1, bf16[4096,1280]{1,0:T(8,128)(2,1)} %wd_hbm.1, ...), custom_call_target="tpu_custom_call" | custom-call | tf_op jit(solution)/shard_map/fused_step/pallas_call | solution.py:689
  73.2 1.7 %copy.15 = bf16[128,1280]{1,0:T(8,128)(2,1)} copy(bf16[128,1280]{1,0:T(8,128)(2,1)} %get-tuple-element.6) | data formatting | bytes 655360
  74.9 2.0 %copy.16 = bf16[1,2560,128]{2,1,0:T(8,128)(2,1)} copy(bf16[1,2560,128]{2,1,0:T(8,128)(2,1)} %get-tuple-element.7) | data formatting | bytes 1310720
  76.9 2.0 %copy.17 = bf16[1,128,2560]{2,1,0:T(8,128)(2,1)} copy(bf16[1,128,2560]{2,1,0:T(8,128)(2,1)} %get-tuple-element.8) | data formatting | bytes 1310720

commit v4 on v3

--- a/solution.py
+++ b/solution.py
@@ -116,9 +116,10 @@
 SLOTS = 40
 TILE = 256
 LANES = 128
-SKEW = 2
+SKEW = 3
 DISPATCH_STEP = 2
-CHILD_STEP = 12
+GATE_STEP = 6
+CHILD_STEP = 15
 BF16 = jnp.bfloat16
 F32 = jnp.float32
 
@@ -208,8 +209,8 @@
     def at(o):
         return lax.rem(e + o, OWN)
 
+    act_load = pltpu.make_async_copy(act_hbm, act, small_sem.at[0])
     small = [
-        pltpu.make_async_copy(act_hbm, act, small_sem.at[0]),
         pltpu.make_async_copy(blocks_hbm, blocks, small_sem.at[1]),
         pltpu.make_async_copy(owner_hbm, owner, small_sem.at[2]),
         pltpu.make_async_copy(cbias_hbm, cbias, small_sem.at[3]),
@@ -235,8 +236,7 @@
         source = wd_hbm.at[pl.ds(pl.multiple_of(g * TILE, TILE), TILE), :]
         return pltpu.make_async_copy(source, wd_buf.at[g], wd_sem.at[g])
 
-    for load in small + gate_loads:
-        load.start()
+    act_load.start()
 
     @pl.loop(0, half + SKEW * last)
     def _(s):
@@ -250,8 +250,8 @@
         def _():
             w_load(down).start()
 
-    enc_load.start()
-    dec_load.start()
+    for load in small + gate_loads + [enc_load, dec_load]:
+        load.start()
     for t in range(half):
         wd_load(t).start()
         wd_load(half + t).start()
@@ -265,6 +265,133 @@
                 )
     pl.semaphore_signal(barrier, inc=1, device_id={"parent": 1 - p})
     acc[...] = jnp.zeros_like(acc)
+    pl.semaphore_wait(barrier, 2 * OWN)
+    act_load.wait()
+
+    def put(ref, value):
+        ref[0:SLOTS, :] = value[:, 0:LANES]
+        ref[SLOTS : 2 * SLOTS, :] = value[:, LANES : 2 * LANES]
+
+    def slot_copy(o, pack_ref, slots_ref, send_sem, recv_sem):
+        return pltpu.make_async_remote_copy(
+            src_ref=pack_ref,
+            dst_ref=slots_ref,
+            send_sem=send_sem,
+            recv_sem=recv_sem,
+            device_id={"expert": at(o), "dp": home},
+        )
+
+    def unless_local(o, action):
+        if o:
+            action()
+        else:
+            pl.when(home != d)(action)
+
+    def is_remote(c, i):
+        return jnp.logical_or(c != d, 2 * d + i != e)
+
+    def gather(ref, c, i):
+        pieces = []
+        for t in range(col_tiles):
+            pieces.append(ref[c, i, t, 0:SLOTS, :].astype(F32))
+            pieces.append(ref[c, i, t, SLOTS : 2 * SLOTS, :].astype(F32))
+        return jnp.concatenate(pieces, axis=1)
+
+    def neighbour(g, move, source, target, send_sems, recv_sems):
+        return pltpu.make_async_remote_copy(
+            src_ref=source.at[g],
+            dst_ref=target.at[g],
+            send_sem=send_sems.at[g],
+            recv_sem=recv_sems.at[g],
+            device_id={"expert": jnp.clip(e + move, 0, last)},
+        )
+
+    def rs_copy(g, move):
+        return neighbour(g, move, rs_send, rs_recv, rs_send_sem, rs_recv_sem)
+
+    def pa_copy(g, move):
+        return neighbour(g, move, pa, pa, pa_send_sem, pa_recv_sem)
+
+    def reduce_tile(g, move, first, end):
+        w_load(g).wait()
+        part[...] = matmul(act[...], w_buf[g])
+
+        @pl.when(e == first)
+        def _():
+            rs_send[g] = part[...].astype(BF16)
+
+        @pl.when(e != first)
+        def _():
+            rs_copy(g, move).wait_recv()
+            value = part[...] + rs_recv[g].astype(F32)
+
+            @pl.when(e != end)
+            def _():
+                rs_send[g] = value.astype(BF16)
+
+            @pl.when(e == end)
+            def _():
+                pa[g] = jnp.maximum(value + bias[g], 0.0).astype(BF16)
+
+        @pl.when(e != end)
+        def _():
+            rs_copy(g, move).start()
+
+    def receive_tile(g, move, first, end):
+        @pl.when(e != first)
+        def _():
+            pa_copy(g, move).wait_recv()
+
+        @pl.when(e != end)
+        def _():
+            pa_copy(g, move).start()
+
+    def use_tile(g):
+        wd_load(g).wait()
+        acc[...] += matmul(pa[g], wd_buf[g])
+
+    def within(t):
+        return jnp.logical_and(t >= 0, t < half)
+
+    def step(s):
+        up, down = s - SKEW * e, s - SKEW * (last - e)
+        back_down, back_up = s - SKEW * (last + e), s - SKEW * (2 * last - e)
+
+        @pl.when(within(up))
+        def _():
+            reduce_tile(half + up, 1, 0, last)
+
+        @pl.when(within(down))
+        def _():
+            reduce_tile(down, -1, last, 0)
+
+        @pl.when(within(back_down))
+        def _():
+            receive_tile(back_down, 1, 0, last)
+
+        @pl.when(within(back_up))
+        def _():
+            receive_tile(half + back_up, -1, last, 0)
+
+        @pl.when(within(back_down))
+        def _():
+            use_tile(back_down)
+
+        @pl.when(within(back_up))
+        def _():
+            use_tile(half + back_up)
+
+    def to_core(source, target, n):
+        return pltpu.make_async_remote_copy(
+            src_ref=source,
+            dst_ref=target,
+            send_sem=core_send_sem.at[n],
+            recv_sem=core_recv_sem.at[n],
+            device_id={"dp": 1 - d},
+        )
+
+    pl.loop(0, DISPATCH_STEP)(step)
+
     for load in small:
         load.wait()
 
@@ -286,6 +413,23 @@
         sel[o] = pick.astype(BF16)
     sel_all[...] = jnp.concatenate([picks[(OWN - q) % OWN] for q in range(OWN)], 0).astype(BF16)
 
+    x_sends = []
+    for o in (2, 1, 3, 0):
+        for t in range(col_tiles):
+            value = matmul(sel[o], act[:, t * TILE : (t + 1) * TILE]).astype(BF16)
+            put(pack.at[o, t], value)
+        copy = slot_copy(
+            o, pack.at[o], x_slots.at[d, side], pack_sem.at[o], x_recv_sem.at[d, side]
+        )
+        unless_local(o, copy.start)
+        x_sends.append((o, copy))
+
+    @pl.when(home == d)
+    def _():
+        x_slots[d, side] = pack[0]
+
+    pl.loop(DISPATCH_STEP, GATE_STEP)(step)
+
     gates = jnp.zeros((8, rows), F32)
     gate_row = lax.broadcasted_iota(jnp.int32, (8, rows), 0)
     for j in range(OWN):
@@ -293,8 +437,6 @@
         first = matmul(act[...], gate_w[j])
         gates = gates + jnp.where(gate_row == j, first.T[0:1], 0.0)
     gate_send[...] = gates
-
-    pl.semaphore_wait(barrier, 2 * OWN)
 
     gate_copies = []
     for o in (1, 2, 3):
@@ -308,145 +450,7 @@
         copy.start()
         gate_copies.append(copy)
 
-    def put(ref, value):
-        ref[0:SLOTS, :] = value[:, 0:LANES]
-        ref[SLOTS : 2 * SLOTS, :] = value[:, LANES : 2 * LANES]
-
-    def slot_copy(o, pack_ref, slots_ref, send_sem, recv_sem):
-        return pltpu.make_async_remote_copy(
-            src_ref=pack_ref,
-            dst_ref=slots_ref,
-            send_sem=send_sem,
-            recv_sem=recv_sem,
-            device_id={"expert": at(o), "dp": home},
-        )
-
-    def unless_local(o, action):
-        if o:
-            action()
-        else:
-            pl.when(home != d)(action)
-
-    def is_remote(c, i):
-        return jnp.logical_or(c != d, 2 * d + i != e)
-
-    def gather(ref, c, i):
-        pieces = []
-        for t in range(col_tiles):
-            pieces.append(ref[c, i, t, 0:SLOTS, :].astype(F32))
-            pieces.append(ref[c, i, t, SLOTS : 2 * SLOTS, :].astype(F32))
-        return jnp.concatenate(pieces, axis=1)
-
-    def neighbour(g, move, source, target, send_sems, recv_sems):
-        return pltpu.make_async_remote_copy(
-            src_ref=source.at[g],
-            dst_ref=target.at[g],
-            send_sem=send_sems.at[g],
-            recv_sem=recv_sems.at[g],
-            device_id={"expert": jnp.clip(e + move, 0, last)},
-        )
-
-    def rs_copy(g, move):
-        return neighbour(g, move, rs_send, rs_recv, rs_send_sem, rs_recv_sem)
-
-    def pa_copy(g, move):
-        return neighbour(g, move, pa, pa, pa_send_sem, pa_recv_sem)
-
-    def reduce_tile(g, move, first, end):
-        w_load(g).wait()
-        part[...] = matmul(act[...], w_buf[g])
-
-        @pl.when(e == first)
-        def _():
-            rs_send[g] = part[...].astype(BF16)
-
-        @pl.when(e != first)
-        def _():
-            rs_copy(g, move).wait_recv()
-            value = part[...] + rs_recv[g].astype(F32)
-
-            @pl.when(e != end)
-            def _():
-                rs_send[g] = value.astype(BF16)
-
-            @pl.when(e == end)
-            def _():
-                pa[g] = jnp.maximum(value + bias[g], 0.0).astype(BF16)
-
-        @pl.when(e != end)
-        def _():
-            rs_copy(g, move).start()
-
-    def receive_tile(g, move, first, end):
-        @pl.when(e != first)
-        def _():
-            pa_copy(g, move).wait_recv()
-
-        @pl.when(e != end)
-        def _():
-            pa_copy(g, move).start()
-
-    def use_tile(g):
-        wd_load(g).wait()
-        acc[...] += matmul(pa[g], wd_buf[g])
-
-    def within(t):
-        return jnp.logical_and(t >= 0, t < half)
-
-    def step(s):
-        up, down = s - SKEW * e, s - SKEW * (last - e)
-        back_down, back_up = s - SKEW * (last + e), s - SKEW * (2 * last - e)
-
-        @pl.when(within(up))
-        def _():
-            reduce_tile(half + up, 1, 0, last)
-
-        @pl.when(within(down))
-        def _():
-            reduce_tile(down, -1, last, 0)
-
-        @pl.when(within(back_down))
-        def _():
-            receive_tile(back_down, 1, 0, last)
-
-        @pl.when(within(back_up))
-        def _():
-            receive_tile(half + back_up, -1, last, 0)
-
-        @pl.when(within(back_down))
-        def _():
-            use_tile(back_down)
-
-        @pl.when(within(back_up))
-        def _():
-            use_tile(half + back_up)
-
-    def to_core(source, target, n):
-        return pltpu.make_async_remote_copy(
-            src_ref=source,
-            dst_ref=target,
-            send_sem=core_send_sem.at[n],
-            recv_sem=core_recv_sem.at[n],
-            device_id={"dp": 1 - d},
-        )
-
-    pl.loop(0, DISPATCH_STEP)(step)
-    x_sends = []
-    for o in (2, 1, 3, 0):
-        for t in range(col_tiles):
-            value = matmul(sel[o], act[:, t * TILE : (t + 1) * TILE]).astype(BF16)
-            put(pack.at[o, t], value)
-        copy = slot_copy(
-            o, pack.at[o], x_slots.at[d, side], pack_sem.at[o], x_recv_sem.at[d, side]
-        )
-        unless_local(o, copy.start)
-        x_sends.append((o, copy))
-
-    @pl.when(home == d)
-    def _():
-        x_slots[d, side] = pack[0]
-
-    pl.loop(DISPATCH_STEP, CHILD_STEP)(step)
+    pl.loop(GATE_STEP, CHILD_STEP)(step)
 
     for c in range(2):
         for i in range(2):

time: 79.1 us -> 79.2 us (level)
  no operation moved by 1% of the time
where the time goes in v4:
time: 79.2 us; the launch traced here: 79 us
  Pallas kernels  72.7 us (92%)
  local copies, waits for them, and re-layouts  5.65 us (7%)
    pallas_call x1, Pallas kernels, fused_body(): pl.pallas_call(fused_kernel, out_shape=(jax.ShapeDtypeStruct((rows, width...  72.7 us
    unnamed x3, local copies, waits for them, and re-layouts  5.65 us

profile of v4, /device:TPU:0, one launch (start us, length us, event | category | flops | bytes accessed | tf_op | source)
XLA Modules:
  0.0 79.0 jit_solution(13373204449496898887)
XLA Ops:
  0.6 72.7 %fused_step.1 = (bf16[128,1280]{1,0:T(8,128)(2,1)}, bf16[1,2560,128]{2,1,0:T(8,128)(2,1)}, bf16[1,128,2560]{2,1,0:T(8,128)(2,1)}) custom-call(s32[8]{0:T(128)} %owner_hbm.1, bf16[128,1280]{1,0:T(8,128)(2,1)} %act_hbm.1, bf16[1280,4096]{1,0:T(8,128)(2,1)} %w_hbm.1, f32[4096]{0:T(1024)} %bias_hbm.1, bf16[4096,1280]{1,0:T(8,128)(2,1)} %wd_hbm.1, ...), custom_call_target="tpu_custom_call" | custom-call | tf_op jit(solution)/shard_map/fused_step/pallas_call | solution.py:693
  73.3 1.7 %copy.15 = bf16[128,1280]{1,0:T(8,128)(2,1)} copy(bf16[128,1280]{1,0:T(8,128)(2,1)} %get-tuple-element.6) | data formatting | bytes 655360
  75.0 2.0 %copy.16 = bf16[1,2560,128]{2,1,0:T(8,128)(2,1)} copy(bf16[1,2560,128]{2,1,0:T(8,128)(2,1)} %get-tuple-element.7) | data formatting | bytes 1310720
  77.0 2.0 %copy.17 = bf16[1,128,2560]{2,1,0:T(8,128)(2,1)} copy(bf16[1,128,2560]{2,1,0:T(8,128)(2,1)} %get-tuple-element.8) | data formatting | bytes 1310720
